TPU v7x, 32 devices: a whole 2x2x4 slice. The times are simulated.
32 devices in a mesh: seq: 8 (over z, x), doc: 4 (over y, core).
Axes of the slice: x: 2, y: 2, z: 4, core: 2. Of those that a mesh axis runs over, the one named last changes fastest.
Arguments:
- queries: bfloat16 [4096, 2048], P(('doc', 'seq')), parts along dimension 0, may hold values from -5 to 5
- key_rows: bfloat16 [4096, 2048], P(('doc', 'seq')), parts along dimension 0, may hold values from -5 to 5
- value_rows: bfloat16 [4096, 2048], P(('doc', 'seq')), parts along dimension 0, may hold values from -6 to 6
- out_grad: bfloat16 [4096, 2048], P(('doc', 'seq')), parts along dimension 0, may hold values from -6 to 6
- vertical: int32 [64, 6], P('doc'), parts along dimension 0, may hold values from 0 to 7, as said below
- slash_offsets: int32 [64, 6], P('doc'), parts along dimension 0, may hold values from -7 to 7, as said below
- counts: int32 [64, 2], P('doc'), parts along dimension 0, may hold values from 1 to 6, as said below
Outputs:
- query_grad: bfloat16 [4096, 2048], P(('doc', 'seq')), parts along dimension 0
- key_grad: bfloat16 [4096, 2048], P(('doc', 'seq')), parts along dimension 0
- value_grad: bfloat16 [4096, 2048], P(('doc', 'seq')), parts along dimension 0
There are 4 independent parts, one for each index of `doc`. A program takes and returns all parts, laid end to end along the dimension named above; each array names one. Nothing has to cross between parts.
Inputs may be any that keep to these rules, and one draw needn't show every extreme that they name: counts[h, 0] is 1 to 6 and counts[h, 1] is 1 to 6; some head has both at their most and some head both at 1. `vertical`: the entries of a head are distinct. `slash_offsets`: the entries of a head are distinct and slash_offsets[h, 0] is 0 for every head.
All inputs are finite; a program needn't handle non-finite values.
Results may differ from a plain program's by a relative error of at most 0.0086.
Values may be sent and summed in bfloat16 or wider, within the bound.
A program may use at most 64 MiB of HBM per device.

v0:
```python
import jax
import jax.numpy as jnp
from jax import lax
from jax.sharding import PartitionSpec as P

HEADS = 16
HEAD_DIM = 128
BLK = 128


block_group = 4


def block_lists(chosen, vert_head, slash_head, count_head, nblocks):
    vert_cap = vert_head.shape[0]
    slash_cap = slash_head.shape[0]
    rows_now = chosen.shape[0]
    vert_index = jnp.broadcast_to(vert_head[None, :], (rows_now, vert_cap))
    vert_valid = jnp.broadcast_to(
        (jnp.arange(vert_cap, dtype=jnp.int32) < count_head[0])[None, :], (rows_now, vert_cap)
    )
    slash_index = chosen[:, None] - slash_head[None, :]
    inside = (slash_index >= 0) & (slash_index < nblocks)
    repeated = jnp.any(
        (vert_index[:, :, None] == slash_index[:, None, :]) & vert_valid[:, :, None], axis=1
    )
    slash_valid = (
        (jnp.arange(slash_cap, dtype=jnp.int32) < count_head[1])[None, :]
        & inside
        & jnp.logical_not(repeated)
    )
    index_table = jnp.clip(jnp.concatenate([vert_index, slash_index], axis=1), 0, nblocks - 1)
    valid_table = jnp.concatenate([vert_valid, slash_valid], axis=1)
    return (index_table, valid_table)


def owner_backward(
    q_blocks, k_blocks, v_blocks, d_blocks, vert_head, slash_head, count_head, chosen_all
):
    nblocks, blk_rows, head_dim = q_blocks.shape
    score_scale = head_dim ** (-0.5)
    vert_cap = vert_head.shape[0]
    trips = count_head[0] + count_head[1]

    def one_group(carried, chosen):
        key_acc, value_acc = carried
        index_table, valid_table = block_lists(chosen, vert_head, slash_head, count_head, nblocks)
        q_group = q_blocks[chosen]
        d_group = d_blocks[chosen]
        group_shape = (chosen.shape[0], blk_rows, 1)

        def fetch(position):
            slot_pick = jnp.where(
                position < count_head[0], position, vert_cap + position - count_head[0]
            )
            column = lax.dynamic_index_in_dim(index_table, slot_pick, 1, keepdims=False)
            usable = lax.dynamic_index_in_dim(valid_table, slot_pick, 1, keepdims=False)[
                :, None, None
            ]
            k_tile = k_blocks[column]
            v_tile = v_blocks[column]
            scores = (
                jnp.einsum("gqd,gkd->gqk", q_group, k_tile, preferred_element_type=jnp.float32)
                * score_scale
            )
            return (column, usable, k_tile, v_tile, scores)

        def row_stats(position, running):
            row_top, row_total = running
            column, usable, k_tile, v_tile, scores = fetch(position)
            new_top = jnp.maximum(
                row_top, jnp.where(usable, jnp.max(scores, axis=-1, keepdims=True), -1e30)
            )
            added = jnp.where(
                usable, jnp.sum(jnp.exp(scores - new_top), axis=-1, keepdims=True), 0.0
            )
            return (new_top, row_total * jnp.exp(row_top - new_top) + added)

        row_top, row_total = lax.fori_loop(
            0,
            trips,
            row_stats,
            (jnp.full(group_shape, -1e30, jnp.float32), jnp.zeros(group_shape, jnp.float32)),
        )

        def probs_of(scores, usable):
            return jnp.where(usable, jnp.exp(scores - row_top) / row_total, 0.0)

        def output_step(position, running):
            column, usable, k_tile, v_tile, scores = fetch(position)
            weights = probs_of(scores, usable).astype(jnp.bfloat16)
            return running + jnp.einsum(
                "gqk,gkd->gqd", weights, v_tile, preferred_element_type=jnp.float32
            )

        attended = lax.fori_loop(
            0, trips, output_step, jnp.zeros((chosen.shape[0], blk_rows, head_dim), jnp.float32)
        )
        row_delta = jnp.sum(d_group.astype(jnp.float32) * attended, axis=-1, keepdims=True)

        def grad_step(position, running):
            query_acc, key_run, value_run = running
            column, usable, k_tile, v_tile, scores = fetch(position)
            probs = probs_of(scores, usable)
            weights = probs.astype(jnp.bfloat16)
            grad_probs = jnp.einsum(
                "gqd,gkd->gqk", d_group, v_tile, preferred_element_type=jnp.float32
            )
            grad_scores = (probs * (grad_probs - row_delta)).astype(jnp.bfloat16)
            query_acc = query_acc + jnp.einsum(
                "gqk,gkd->gqd", grad_scores, k_tile, preferred_element_type=jnp.float32
            )
            key_part = (
                jnp.einsum("gqk,gqd->gkd", grad_scores, q_group, preferred_element_type=jnp.float32)
                * score_scale
            )
            value_part = jnp.einsum(
                "gqk,gqd->gkd", weights, d_group, preferred_element_type=jnp.float32
            )
            return (
                query_acc,
                key_run.at[column].add(key_part),
                value_run.at[column].add(value_part),
            )

        start_query = jnp.zeros((chosen.shape[0], blk_rows, head_dim), jnp.float32)
        query_acc, key_acc, value_acc = lax.fori_loop(
            0, trips, grad_step, (start_query, key_acc, value_acc)
        )
        return ((key_acc, value_acc), query_acc * score_scale)

    zeros_acc = jnp.zeros((nblocks, blk_rows, head_dim), jnp.float32)
    (key_acc, value_acc), query_grad = lax.scan(one_group, (zeros_acc, zeros_acc), chosen_all)
    return (query_grad.reshape(-1, blk_rows, head_dim), key_acc, value_acc)


def body(queries, key_rows, value_rows, out_grad, vertical, slash_offsets, counts):
    tokens_here = queries.shape[0]
    device_count = lax.axis_size("seq")
    device_here = lax.axis_index("seq")
    full_width = HEADS * HEAD_DIM

    def doubled(matrix):
        return jnp.repeat(matrix.reshape(tokens_here, HEADS, HEAD_DIM), 2, axis=1)

    q_owned, k_owned, v_owned, d_owned = (
        lax.all_to_all(doubled(queries), "seq", split_axis=1, concat_axis=0, tiled=True),
        lax.all_to_all(doubled(key_rows), "seq", split_axis=1, concat_axis=0, tiled=True),
        lax.all_to_all(doubled(value_rows), "seq", split_axis=1, concat_axis=0, tiled=True),
        lax.all_to_all(doubled(out_grad), "seq", split_axis=1, concat_axis=0, tiled=True),
    )
    length = tokens_here * device_count
    nblocks = length // BLK
    per_device = 2 * HEADS // device_count
    query_parts = []
    key_parts = []
    value_parts = []
    for local_slot in range(per_device):
        slot_index = device_here * per_device + local_slot
        head_index = slot_index // 2
        parity = slot_index % 2
        chosen_all = (parity + 2 * jnp.arange(nblocks // 2, dtype=jnp.int32)).reshape(
            -1, block_group
        )

        def blockwise(matrix):
            return matrix[:, local_slot, :].reshape(nblocks, BLK, HEAD_DIM)

        query_sel, key_acc, value_acc = owner_backward(
            blockwise(q_owned),
            blockwise(k_owned),
            blockwise(v_owned),
            blockwise(d_owned),
            vertical[head_index],
            slash_offsets[head_index],
            counts[head_index],
            chosen_all,
        )
        query_full = (
            jnp.zeros((nblocks, BLK, HEAD_DIM), jnp.float32)
            .at[chosen_all.reshape(-1)]
            .set(query_sel)
        )
        query_parts.append(query_full.reshape(length, HEAD_DIM))
        key_parts.append(key_acc.reshape(length, HEAD_DIM))
        value_parts.append(value_acc.reshape(length, HEAD_DIM))
    all_parts = (query_parts, key_parts, value_parts)
    stacked = [jnp.stack(member, axis=1) for member in all_parts]
    returned = (
        lax.all_to_all(stacked[0], "seq", split_axis=0, concat_axis=1, tiled=True),
        lax.all_to_all(stacked[1], "seq", split_axis=0, concat_axis=1, tiled=True),
        lax.all_to_all(stacked[2], "seq", split_axis=0, concat_axis=1, tiled=True),
    )
    results = [
        back.reshape(tokens_here, HEADS, 2, HEAD_DIM)
        .sum(axis=2)
        .astype(jnp.bfloat16)
        .reshape(tokens_here, full_width)
        for back in returned
    ]
    return (results[0], results[1], results[2])


def solution(mesh):
    return jax.shard_map(
        body,
        mesh=mesh,
        in_specs=(
            P(("doc", "seq"), None),
            P(("doc", "seq"), None),
            P(("doc", "seq"), None),
            P(("doc", "seq"), None),
            P("doc", None),
            P("doc", None),
            P("doc", None),
        ),
        out_specs=(P(("doc", "seq"), None), P(("doc", "seq"), None), P(("doc", "seq"), None)),
        check_vma=False,
    )
```

profile of v0, /device:TPU:1, one launch (start us, length us, event | category | flops | bytes accessed | tf_op | source)
XLA Modules:
  0.0 750.5 jit_solution(12686768721230638151)
XLA Ops:
  3.2 6.4 all-to-all-start.1
  27.8 6.3 all-to-all-done.1
  35.4 4.9 all-to-all-start
  47.0 18.4 %all-to-all-done = bf16[128,32,128]{2,0,1:T(8,128)(2,1)S(1)} async-done(((bf16[128,32,128]{2,0,1:T(8,128)(2,1)}), bf16[128,32,128]{2,0,1:T(8,128)(2,1)S(1)}, u32[]{:S(2)}, u32[]{:S(2)}) %all-to-all-start) | async-done | bytes 1048608 | tf_op jit(solution)/shard_map/all_to_all | solution.py:148
  66.8 4.5 all-to-all-start.2
  73.4 22.1 %while.216 = (s32[]{:T(128)}, f32[4,128,1]{1,0,2:T(4,128)S(1)}, f32[4,128,1]{1,0,2:T(4,128)S(1)}, s32[]{:T(128)}, s32[2]{0:T(128)}, /*index=5*/pred[4,12]{0,1:T(...) while((s32[]{:T(128)}, f32[4,128,1]{1,0,2:T(4,128)S(1)}, ...), condition=%wide.region_4.5_spmd, body=%wide.region_1.4_spmd.sunk | while | flops 17042452 | bytes 1079589 | solution.py:79
  97.7 10.9 %all-to-all-start.3 = ((bf16[128,32,128]{2,0,1:T(8,128)(2,1)}), bf16[128,32,128]{2,0,1:T(8,128)(2,1)S(1)}, u32[]{:S(2)}, u32[]{:S(2)}) async-start(bf16[128,32,128]{2,0,1:T(8,128)(2,1)} %bitcast.588), calls=%async_computation.3 | async-start | bytes 2097152 | tf_op jit(solution)/shard_map/all_to_all | solution.py:150
  109.8 27.3 %while.217 = (s32[]{:T(128)}, f32[4,128,128]{2,1,0:T(8,128)S(1)}, s32[]{:T(128)}, s32[2]{0:T(128)}, pred[4,12]{0,1:T(8,128)(4,1)S(1)}, /*index=5*/s32[4,12]{0,1:...) while((s32[]{:T(128)}, f32[4,128,128]{2,1,0:T(8,128)S(1)}, ...), condition=%wide.region_6.7_spmd, body=%wide.region_5.6_spmd.sunk | while | flops 33948692 | bytes 1450305 | solution.py:96
  139.1 40.1 %while.218 = (s32[]{:T(128)}, f32[4,128,128]{2,1,0:T(8,128)S(1)}, f32[8,128,128]{2,1,0:T(8,128)S(1)}, f32[8,128,128]{2,1,0:T(8,128)S(1)}, s32[]{:T(128)}, /*inde...) while((s32[]{:T(128)}, f32[4,128,128]{2,1,0:T(8,128)S(1)}, ...), condition=%wide.region_11.12_spmd, body=%wide.region_8.11_spmd.sunk | while | flops 84673552 | bytes 5253505 | solution.py:127
  180.9 10.9 %while.219 = (s32[]{:T(128)}, f32[4,128,1]{1,0,2:T(4,128)S(1)}, f32[4,128,1]{1,0,2:T(4,128)S(1)}, s32[]{:T(128)}, s32[2]{0:T(128)S(1)}, /*index=5*/pred[4,12]{0,...) while((s32[]{:T(128)}, f32[4,128,1]{1,0,2:T(4,128)S(1)}, ...), condition=%wide.region_17.18_spmd, body=%wide.region_14.17_spmd.sunk | while | flops 17042452 | bytes 1079589 | solution.py:79
  191.9 20.2 %while.220 = (s32[]{:T(128)}, f32[4,128,128]{2,1,0:T(8,128)S(1)}, s32[]{:T(128)}, s32[2]{0:T(128)S(1)}, pred[4,12]{0,1:T(8,128)(4,1)S(1)}, /*index=5*/s32[4,12]{...) while((s32[]{:T(128)}, f32[4,128,128]{2,1,0:T(8,128)S(1)}, ...), condition=%wide.region_19.20_spmd, body=%wide.region_18.19_spmd.sunk | while | flops 33948692 | bytes 1450305 | solution.py:96
  214.7 51.6 %while.221 = (s32[]{:T(128)}, f32[4,128,128]{2,1,0:T(8,128)S(1)}, f32[8,128,128]{2,1,0:T(8,128)}, f32[8,128,128]{2,1,0:T(8,128)}, s32[]{:T(128)}, /*index=5*/s32...) while((s32[]{:T(128)}, f32[4,128,128]{2,1,0:T(8,128)S(1)}, ...), condition=%wide.region_24.25_spmd, body=%wide.region_21.24_spmd.sunk | while | flops 84673552 | bytes 5253505 | solution.py:127
  244.0 2.3 scatter_fusion.2
  261.2 2.3 scatter_fusion.2
  268.0 3.6 while.222
  271.7 6.7 while.223
  281.0 17.2 %while.224 = (s32[]{:T(128)}, f32[4,128,128]{2,1,0:T(8,128)S(1)}, f32[8,128,128]{2,1,0:T(8,128)}, f32[8,128,128]{2,1,0:T(8,128)}, s32[]{:T(128)}, /*index=5*/s32...) while((s32[]{:T(128)}, f32[4,128,128]{2,1,0:T(8,128)S(1)}, ...), condition=%wide.region_37.38_spmd, body=%wide.region_34.37_spmd.sunk | while | flops 84673552 | bytes 5253505 | solution.py:127
  284.6 2.3 scatter_fusion.4
  299.9 2.3 while.225
  302.3 5.4 while.226
  310.3 16.1 %while.227 = (s32[]{:T(128)}, f32[4,128,128]{2,1,0:T(8,128)S(1)}, f32[8,128,128]{2,1,0:T(8,128)}, f32[8,128,128]{2,1,0:T(8,128)}, s32[]{:T(128)}, /*index=5*/s32...) while((s32[]{:T(128)}, f32[4,128,128]{2,1,0:T(8,128)S(1)}, ...), condition=%wide.region_50.51_spmd, body=%wide.region_47.50_spmd.sunk | while | flops 84673552 | bytes 5253505 | solution.py:127
  313.1 2.3 scatter_fusion.6
  315.6 2.3 scatter_fusion.7
  326.3 4.6 pad_maximum_fusion.2
  331.0 310.6 %all-to-all-start.6 = ((f32[1024,4,128]{2,1,0:T(4,128)}), f32[1024,4,128]{2,1,0:T(4,128)}, u32[]{:S(2)}, u32[]{:S(2)}) async-start(f32[1024,4,128]{2,1,0:T(4,128)} %pad_maximum_fusion.2), calls=%async_computation.6 | async-start | bytes 4194304 | tf_op jit(solution)/shard_map/all_to_all | solution.py:192
  641.6 4.4 pad_maximum_fusion.1
  646.0 36.9 %all-to-all-done.6 = f32[1024,4,128]{2,1,0:T(4,128)} async-done(((f32[1024,4,128]{2,1,0:T(4,128)}), f32[1024,4,128]{2,1,0:T(4,128)}, u32[]{:S(2)}, u32[]{:S(2)}) %all-to-all-start.6) | async-done | bytes 2097184 | tf_op jit(solution)/shard_map/all_to_all | solution.py:192
  682.9 4.4 all-to-all-start.5
  690.3 3.3 pad_maximum_fusion
  693.7 19.9 %all-to-all-done.5 = f32[1024,4,128]{2,1,0:T(4,128)} async-done(((f32[1024,4,128]{2,1,0:T(4,128)}), f32[1024,4,128]{2,1,0:T(4,128)}, u32[]{:S(2)}, u32[]{:S(2)}) %all-to-all-start.5) | async-done | bytes 2097184 | tf_op jit(solution)/shard_map/all_to_all | solution.py:191
  713.5 4.4 all-to-all-start.4
  730.5 13.6 %all-to-all-done.4 = f32[1024,4,128]{2,1,0:T(4,128)} async-done(((f32[1024,4,128]{2,1,0:T(4,128)}), f32[1024,4,128]{2,1,0:T(4,128)}, u32[]{:S(2)}, u32[]{:S(2)}) %all-to-all-start.4) | async-done | bytes 2097184 | tf_op jit(solution)/shard_map/all_to_all | solution.py:190
  (627 shorter events, 250.9 us)
Async XLA Ops:
  1.8 7.7 %copy-start.12 = (s32[16,6]{0,1:T(8,128)S(1)}, s32[16,6]{0,1:T(8,128)}, u32[]{:S(2)}) copy-start(s32[16,6]{0,1:T(8,128)} %param.36) | copy-start | bytes 1156
  1.8 7.9 %copy-start.14 = (s32[16,2]{0,1:T(2,128)S(1)}, s32[16,2]{0,1:T(2,128)}, u32[]{:S(2)}) copy-start(s32[16,2]{0,1:T(2,128)} %param.37) | copy-start | bytes 388
  1.8 9.9 %copy-start.13 = (s32[16,6]{0,1:T(8,128)S(1)}, s32[16,6]{0,1:T(8,128)}, u32[]{:S(2)}) copy-start(s32[16,6]{0,1:T(8,128)} %param.35) | copy-start | bytes 1156
  1.8 25.8 %copy-start.10 = (bf16[128,2048]{1,0:T(8,128)(2,1)S(1)}, bf16[128,2048]{1,0:T(8,128)(2,1)}, u32[]{:S(2)}) copy-start(bf16[128,2048]{1,0:T(8,128)(2,1)} %param.32) | copy-start | bytes 1572868
  3.2 31.0 %all-to-all-start.1 = ((bf16[128,32,128]{2,0,1:T(8,128)(2,1)}), bf16[128,32,128]{2,0,1:T(8,128)(2,1)S(1)}, u32[]{:S(2)}, u32[]{:S(2)}) async-start(bf16[128,32,128]{2,0,1:T(8,128)(2,1)} %bitcast.80), calls=%async_computation.1 | async-start | bytes 2097152 | tf_op jit(solution)/shard_map/all_to_all | solution.py:147
  27.8 16.1 %copy-start.11 = (bf16[128,2048]{1,0:T(8,128)(2,1)S(1)}, bf16[128,2048]{1,0:T(8,128)(2,1)}, u32[]{:S(2)}) copy-start(bf16[128,2048]{1,0:T(8,128)(2,1)} %param.33) | copy-start | bytes 1572868
  35.4 30.0 %all-to-all-start = ((bf16[128,32,128]{2,0,1:T(8,128)(2,1)}), bf16[128,32,128]{2,0,1:T(8,128)(2,1)S(1)}, u32[]{:S(2)}, u32[]{:S(2)}) async-start(bf16[128,32,128]{2,0,1:T(8,128)(2,1)} %bitcast.590), calls=%async_computation | async-start | bytes 2097152 | tf_op jit(solution)/shard_map/all_to_all | solution.py:148
  42.0 4.0 copy-start.20
  42.0 4.0 copy-start.22
  42.0 4.0 copy-start.16
  42.0 4.0 copy-start.18
  42.0 30.7 %copy-start.15 = (s32[1024]{0:T(1024)}, s32[1024]{0:T(1024)S(1)}, u32[]{:S(2)}) copy-start(s32[1024]{0:T(1024)S(1)} %pad_clamp_fusion.15) | copy-start | bytes 12292
  66.8 29.6 %all-to-all-start.2 = ((bf16[128,32,128]{2,0,1:T(8,128)(2,1)}), bf16[128,32,128]{2,0,1:T(8,128)(2,1)S(1)}, u32[]{:S(2)}, u32[]{:S(2)}) async-start(bf16[128,32,128]{2,0,1:T(8,128)(2,1)} %bitcast.85), calls=%async_computation.2 | async-start | bytes 2097152 | tf_op jit(solution)/shard_map/all_to_all | solution.py:149
  73.4 23.0 %copy-start.5 = (bf16[128,16,128]{2,0,1:T(8,128)(2,1)S(1)}, bf16[128,16,128]{2,0,1:T(8,128)(2,1)}, u32[]{:S(2)}) copy-start(bf16[128,16,128]{2,0,1:T(8,128)(2,1)} %copy_bitcast_fusion) | copy-start | bytes 1572868
  97.7 39.4 %all-to-all-start.3 = ((bf16[128,32,128]{2,0,1:T(8,128)(2,1)}), bf16[128,32,128]{2,0,1:T(8,128)(2,1)S(1)}, u32[]{:S(2)}, u32[]{:S(2)}) async-start(bf16[128,32,128]{2,0,1:T(8,128)(2,1)} %bitcast.588), calls=%async_computation.3 | async-start | bytes 2097152 | tf_op jit(solution)/shard_map/all_to_all | solution.py:150
  139.0 41.8 %copy-start.26 = (pred[4,12]{0,1:T(8,128)(4,1)S(1)}, pred[4,12]{0,1:T(8,128)(4,1)}, u32[]{:S(2)}) copy-start(pred[4,12]{0,1:T(8,128)(4,1)} %copy.175) | copy-start | bytes 148
  139.0 41.8 %copy-start.30 = (s32[2]{0:T(128)S(1)}, s32[2]{0:T(128)}, u32[]{:S(2)}) copy-start(s32[2]{0:T(128)} %get-tuple-element.2954) | copy-start | bytes 28
  191.8 20.3 %copy-start.8 = (bf16[1024,1,128]{2,0,1:T(8,128)(2,1)S(1)}, bf16[1024,1,128]{2,0,1:T(8,128)(2,1)}, u32[]{:S(2)}) copy-start(bf16[1024,1,128]{2,0,1:T(8,128)(2,1)} %get-tuple-element.1664) | copy-start | bytes 786436
  214.7 53.3 %copy-start.25 = (pred[4,12]{0,1:T(8,128)(4,1)S(1)}, pred[4,12]{0,1:T(8,128)(4,1)}, u32[]{:S(2)}) copy-start(pred[4,12]{0,1:T(8,128)(4,1)} %copy.181) | copy-start | bytes 148
  214.7 53.3 %copy-start.29 = (s32[2]{0:T(128)S(1)}, s32[2]{0:T(128)}, u32[]{:S(2)}) copy-start(s32[2]{0:T(128)} %get-tuple-element.2813) | copy-start | bytes 28
  271.7 6.8 copy-start.7
  281.0 18.9 %copy-start.24 = (pred[4,12]{0,1:T(8,128)(4,1)S(1)}, pred[4,12]{0,1:T(8,128)(4,1)}, u32[]{:S(2)}) copy-start(pred[4,12]{0,1:T(8,128)(4,1)} %copy.187) | copy-start | bytes 148
  281.0 18.9 %copy-start.28 = (s32[2]{0:T(128)S(1)}, s32[2]{0:T(128)}, u32[]{:S(2)}) copy-start(s32[2]{0:T(128)} %get-tuple-element.2672) | copy-start | bytes 28
  302.3 5.4 copy-start.6
  331.0 310.6 %copy-start.2 = (f32[8,128,128]{2,1,0:T(8,128)S(1)}, f32[8,128,128]{2,1,0:T(8,128)}, u32[]{:S(2)}) copy-start(f32[8,128,128]{2,1,0:T(8,128)} %get-tuple-element.924) | copy-start | bytes 1572868
  331.0 310.6 %copy-start.3 = (f32[8,128,128]{2,1,0:T(8,128)S(1)}, f32[8,128,128]{2,1,0:T(8,128)}, u32[]{:S(2)}) copy-start(f32[8,128,128]{2,1,0:T(8,128)} %get-tuple-element.925) | copy-start | bytes 1572868
  331.0 351.9 %all-to-all-start.6 = ((f32[1024,4,128]{2,1,0:T(4,128)}), f32[1024,4,128]{2,1,0:T(4,128)}, u32[]{:S(2)}, u32[]{:S(2)}) async-start(f32[1024,4,128]{2,1,0:T(4,128)} %pad_maximum_fusion.2), calls=%async_computation.6 | async-start | bytes 4194304 | tf_op jit(solution)/shard_map/all_to_all | solution.py:192
  646.0 41.4 %copy-start.23 = (s32[4]{0:T(128)S(1)}, s32[4]{0:T(128)}, u32[]{:S(2)}) copy-start(s32[4]{0:T(128)} %copy-done.22) | copy-start | bytes 52
  682.9 30.6 %all-to-all-start.5 = ((f32[1024,4,128]{2,1,0:T(4,128)}), f32[1024,4,128]{2,1,0:T(4,128)}, u32[]{:S(2)}, u32[]{:S(2)}) async-start(f32[1024,4,128]{2,1,0:T(4,128)} %pad_maximum_fusion.1), calls=%async_computation.5 | async-start | bytes 4194304 | tf_op jit(solution)/shard_map/all_to_all | solution.py:191
  687.4 1.6 copy-start.19
  713.5 30.6 %all-to-all-start.4 = ((f32[1024,4,128]{2,1,0:T(4,128)}), f32[1024,4,128]{2,1,0:T(4,128)}, u32[]{:S(2)}, u32[]{:S(2)}) async-start(f32[1024,4,128]{2,1,0:T(4,128)} %pad_maximum_fusion), calls=%async_computation.4 | async-start | bytes 4194304 | tf_op jit(solution)/shard_map/all_to_all | solution.py:190
  747.3 3.2 copy-start.1
  (6 other events, 7.3 us)
where the time goes:
time: 753 us; the launch traced here: 750 us
  starting transfers between devices  346 us (46%)
  local copies, waits for them, and re-layouts  132 us (18%)
  other arithmetic  114 us (15%)
  waiting for transfers between devices  96.1 us (13%)
  loops' own time  27.8 us (4%)
  matrix products  27 us (4%)
    all_to_all x1, starting transfers between devices, body(): lax.all_to_all(stacked[2], 'seq', split_axis=0, concat_axis=1, tiled=True)  311 us
    gather x32, local copies, waits for them, and re-layouts, fetch(): v_tile = v_blocks[column]  48.7 us
    all_to_all x1, waiting for transfers between devices, body(): lax.all_to_all(stacked[2], 'seq', split_axis=0, concat_axis=1, tiled=True)  36.9 us
    select_n x48, other arithmetic, fetch(): k_tile = k_blocks[column]  29.1 us
    scatter-add x16, other arithmetic, grad_step(): key_run.at[column].add(key_part)  27.6 us
    scatter-add x16, other arithmetic, grad_step(): value_run.at[column].add(value_part)  27.5 us
    gather x48, local copies, waits for them, and re-layouts, fetch(): k_tile = k_blocks[column]  27.4 us
    all_to_all x1, waiting for transfers between devices, body(): lax.all_to_all(stacked[1], 'seq', split_axis=0, concat_axis=1, tiled=True)  19.9 us
  transfers between devices with their start and end apart: 7, of which 6 were waited for; matrix products, arithmetic and copies ran while one was open for 11% of the time, Pallas kernels for 0%

commit v1 on v0

--- a/solution.py
+++ b/solution.py
@@ -1,6 +1,10 @@
+import functools
+
 import jax
 import jax.numpy as jnp
 from jax import lax
+from jax.experimental import pallas as pl
+from jax.experimental.pallas import tpu as pltpu
 from jax.sharding import PartitionSpec as P
 
 HEADS = 16
@@ -134,7 +138,7 @@
     return (query_grad.reshape(-1, blk_rows, head_dim), key_acc, value_acc)
 
 
-def body(queries, key_rows, value_rows, out_grad, vertical, slash_offsets, counts):
+def split_head_body(queries, key_rows, value_rows, out_grad, vertical, slash_offsets, counts):
     tokens_here = queries.shape[0]
     device_count = lax.axis_size("seq")
     device_here = lax.axis_index("seq")
@@ -201,9 +205,367 @@
     return (results[0], results[1], results[2])
 
 
+MESH = pl.DeviceIdType.MESH
+QUERY_TILE = 256
+LOG2E = 1.4426950408889634
+NEVER = -1e30
+
+
+def fused_kernel(
+    count,
+    slots,
+    k_in,
+    v_in,
+    q_in,
+    d_in,
+    vertical,
+    slash_offsets,
+    counts,
+    dq_parts,
+    dk_out,
+    dv_out,
+    kv_here,
+    qd_here,
+    dkv_done,
+    dq_done,
+    bias,
+    stats,
+    partner_stats,
+    key_acc,
+    value_acc,
+    kv_send,
+    kv_recv,
+    qd_send,
+    qd_recv,
+    own_in,
+    stat_send,
+    stat_recv,
+    dkv_send,
+    dkv_recv,
+    dq_send,
+    dq_recv,
+    own_back,
+):
+    me = lax.axis_index("seq")
+    near = count // 2
+    half = me // near
+    group = me % near
+    first = half * near
+    length = count * BLK
+    score_scale = HEAD_DIM ** (-0.5)
+    kv_sources = (k_in, v_in)
+    qd_sources = (q_in, d_in)
+    dkv_targets = (dk_out, dv_out)
+
+    def offset_of(step):
+        return count // 2 + ((step + 1) // 2) * (2 * (step % 2) - 1)
+
+    def rows_of(index):
+        return pl.ds(pl.multiple_of(index * BLK, BLK), BLK)
+
+    def columns_of(owner_group, slot):
+        return pl.ds(pl.multiple_of((owner_group * slots + slot) * HEAD_DIM, HEAD_DIM), HEAD_DIM)
+
+    def far_pair(step):
+        offset = offset_of(step)
+        return (me + offset) % count, (me + count - offset) % count
+
+    def near_pair(step):
+        return (group + 1 + step) % near, (group + near - 1 - step) % near
+
+    def remote(src, dst, send_sem, recv_sem, peer):
+        return pltpu.make_async_remote_copy(
+            src_ref=src,
+            dst_ref=dst,
+            send_sem=send_sem,
+            recv_sem=recv_sem,
+            device_id={"seq": peer},
+            device_id_type=MESH,
+        )
+
+    def send_qd(which, slot, step, sending):
+        peer, source = far_pair(step)
+        return remote(
+            qd_sources[which].at[:, columns_of(peer % near, slot)],
+            qd_here.at[which, slot, rows_of(me if sending else source), :],
+            qd_send.at[which, slot, step],
+            qd_recv.at[which, slot, step],
+            peer,
+        )
+
+    def send_kv(which, slot, step, sending):
+        peer, source = near_pair(step)
+        return remote(
+            kv_sources[which].at[:, columns_of(peer, slot)],
+            kv_here.at[which, slot, rows_of(group if sending else source), :],
+            kv_send.at[which, slot, step],
+            kv_recv.at[which, slot, step],
+            first + peer,
+        )
+
+    def own_copies(slot):
+        here = columns_of(group, slot)
+        pairs = [
+            (kv_sources[which].at[:, here], kv_here.at[which, slot, rows_of(group), :])
+            for which in range(2)
+        ] + [
+            (qd_sources[which].at[:, here], qd_here.at[which, slot, rows_of(me), :])
+            for which in range(2)
+        ]
+        return [
+            pltpu.make_async_copy(src, dst, own_in.at[index, slot])
+            for index, (src, dst) in enumerate(pairs)
+        ]
+
+    def send_stats(slot):
+        return remote(
+            stats.at[slot],
+            partner_stats.at[slot],
+            stat_send.at[slot],
+            stat_recv.at[slot],
+            (me + near) % count,
+        )
+
+    def back_dq(slot, step, sending):
+        peer, source = far_pair(step)
+        origin = me if sending else source
+        return remote(
+            dq_done.at[slot, rows_of(peer), :],
+            dq_parts.at[rows_of(origin // near), columns_of(origin % near, slot)],
+            dq_send.at[slot, step],
+            dq_recv.at[slot, step],
+            peer,
+        )
+
+    def back_dkv(which, slot, step, sending):
+        peer, source = near_pair(step)
+        return remote(
+            dkv_done.at[which, slot, rows_of(peer), :],
+            dkv_targets[which].at[:, columns_of(group if sending else source, slot)],
+            dkv_send.at[which, slot, step],
+            dkv_recv.at[which, slot, step],
+            first + peer,
+        )
+
+    def own_returns(slot):
+        here = columns_of(group, slot)
+        pairs = [
+            (dkv_done.at[which, slot, rows_of(group), :], dkv_targets[which].at[:, here])
+            for which in range(2)
+        ] + [(dq_done.at[slot, rows_of(me), :], dq_parts.at[rows_of(half), here])]
+        return [
+            pltpu.make_async_copy(src, dst, own_back.at[index, slot])
+            for index, (src, dst) in enumerate(pairs)
+        ]
+
+    barrier = pltpu.get_barrier_semaphore()
+
+    @pl.loop(1, count)
+    def _(step):
+        pl.semaphore_signal(
+            barrier, inc=1, device_id={"seq": (me + step) % count}, device_id_type=MESH
+        )
+
+    pl.semaphore_wait(barrier, count - 1)
+
+    for slot in range(slots):
+
+        @pl.loop(0, count - 1)
+        def _(step, slot=slot):
+            for which in range(2):
+                send_qd(which, slot, step, True).start()
+
+        @pl.loop(0, near - 1)
+        def _(step, slot=slot):
+            for which in range(2):
+                send_kv(which, slot, step, True).start()
+
+        for copy in own_copies(slot):
+            copy.start()
+
+    key_block = first + lax.broadcasted_iota(jnp.int32, (near, length), 0)
+    query_block = lax.broadcasted_iota(jnp.int32, (near, length), 1) // BLK
+    for slot in range(slots):
+        head = group * slots + slot
+        allowed = jnp.zeros((near, length), jnp.float32)
+        for entry in range(vertical.shape[0]):
+            wanted = jnp.where(entry < counts[0, head], vertical[entry, head], -1)
+            allowed = jnp.where(key_block == wanted, 1.0, allowed)
+        for entry in range(slash_offsets.shape[0]):
+            wanted = jnp.where(entry < counts[1, head], slash_offsets[entry, head], 2 * count)
+            allowed = jnp.where(query_block - key_block == wanted, 1.0, allowed)
+        bias[slot] = jnp.where(allowed > 0.0, 0.0, NEVER)
+
+    def dot(a, b, a_dim, b_dim):
+        return lax.dot_general(
+            a, b, (((a_dim,), (b_dim,)), ((), ())), preferred_element_type=jnp.float32
+        )
+
+    def tile_range(tile):
+        return pl.ds(pl.multiple_of(tile * QUERY_TILE, QUERY_TILE), QUERY_TILE)
+
+    def scores_of(slot, here):
+        mask = jnp.concatenate(
+            [
+                jnp.broadcast_to(bias[slot, part : part + 1, here], (BLK, QUERY_TILE))
+                for part in range(near)
+            ],
+            axis=0,
+        )
+        products = dot(kv_here[0, slot], qd_here[0, slot, here, :], 1, 1)
+        return products * (score_scale * LOG2E) + mask
+
+    def first_phase(slot):
+        @pl.loop(0, count - 1)
+        def _(step):
+            for which in range(2):
+                send_qd(which, slot, step, False).wait_recv()
+
+        @pl.loop(0, near - 1)
+        def _(step):
+            for which in range(2):
+                send_kv(which, slot, step, False).wait_recv()
+
+        for copy in own_copies(slot):
+            copy.wait()
+
+        @pl.loop(0, length // QUERY_TILE)
+        def _(tile):
+            here = tile_range(tile)
+            scores = scores_of(slot, here)
+            top = jnp.max(scores, axis=0, keepdims=True)
+            raised = jnp.exp2(scores - top)
+            grad_probs = dot(kv_here[1, slot], qd_here[1, slot, here, :], 1, 1)
+            stats[slot, 0, :, here] = top
+            stats[slot, 1, :, here] = jnp.sum(raised, axis=0, keepdims=True)
+            stats[slot, 2, :, here] = jnp.sum(raised * grad_probs, axis=0, keepdims=True)
+
+        send_stats(slot).start()
+
+    def second_phase(slot):
+        send_stats(slot).wait_recv()
+        key_acc[...] = jnp.zeros_like(key_acc)
+        value_acc[...] = jnp.zeros_like(value_acc)
+
+        @pl.loop(0, length // QUERY_TILE)
+        def _(tile):
+            here = tile_range(tile)
+            keys = kv_here[0, slot]
+            q_tile = qd_here[0, slot, here, :]
+            d_tile = qd_here[1, slot, here, :]
+            my_top = stats[slot, 0, :, here]
+            its_top = partner_stats[slot, 0, :, here]
+            top = jnp.maximum(my_top, its_top)
+            mine = jnp.exp2(my_top - top)
+            its = jnp.exp2(its_top - top)
+            inverse = 1.0 / (stats[slot, 1, :, here] * mine + partner_stats[slot, 1, :, here] * its)
+            row_delta = inverse * (
+                stats[slot, 2, :, here] * mine + partner_stats[slot, 2, :, here] * its
+            )
+            probs = jnp.exp2(scores_of(slot, here) - top) * inverse
+            weights = probs.astype(jnp.bfloat16)
+            grad_probs = dot(kv_here[1, slot], d_tile, 1, 1)
+            grad_scores = (probs * (grad_probs - row_delta)).astype(jnp.bfloat16)
+            dq_done[slot, here, :] = (dot(keys, grad_scores, 0, 0) * score_scale).T.astype(
+                jnp.bfloat16
+            )
+            key_acc[...] += dot(grad_scores, q_tile, 1, 0)
+            value_acc[...] += dot(weights, d_tile, 1, 0)
+
+        dkv_done[0, slot] = (key_acc[...] * score_scale).astype(jnp.bfloat16)
+        dkv_done[1, slot] = value_acc[...].astype(jnp.bfloat16)
+
+        @pl.loop(0, count - 1)
+        def _(step):
+            back_dq(slot, step, True).start()
+
+        @pl.loop(0, near - 1)
+        def _(step):
+            for which in range(2):
+                back_dkv(which, slot, step, True).start()
+
+        for copy in own_returns(slot):
+            copy.start()
+
+    for slot in range(slots):
+        first_phase(slot)
+        if slot > 0:
+            second_phase(slot - 1)
+    second_phase(slots - 1)
+
+    for slot in range(slots):
+
+        @pl.loop(0, count - 1)
+        def _(step, slot=slot):
+            for which in range(2):
+                send_qd(which, slot, step, True).wait_send()
+            back_dq(slot, step, True).wait_send()
+            back_dq(slot, step, False).wait_recv()
+
+        @pl.loop(0, near - 1)
+        def _(step, slot=slot):
+            for which in range(2):
+                send_kv(which, slot, step, True).wait_send()
+                back_dkv(which, slot, step, True).wait_send()
+                back_dkv(which, slot, step, False).wait_recv()
+
+        send_stats(slot).wait_send()
+        for copy in own_returns(slot):
+            copy.wait()
+
+
+def whole_head_body(queries, key_rows, value_rows, out_grad, vertical, slash_offsets, counts):
+    count = lax.axis_size("seq")
+    near = count // 2
+    slots = HEADS // near
+    length = count * BLK
+    kept = near * BLK
+    anywhere = pl.BlockSpec(memory_space=pl.ANY)
+    scalars = pl.BlockSpec(memory_space=pltpu.SMEM)
+    shape = jax.ShapeDtypeStruct(queries.shape, queries.dtype)
+    parts = jax.ShapeDtypeStruct((2 * queries.shape[0], queries.shape[1]), queries.dtype)
+    sems = pltpu.SemaphoreType.DMA
+    dq_parts, key_grad, value_grad = pl.pallas_call(
+        functools.partial(fused_kernel, count, slots),
+        out_shape=(parts, shape, shape),
+        in_specs=[anywhere] * 4 + [scalars] * 3,
+        out_specs=(anywhere, anywhere, anywhere),
+        scratch_shapes=[
+            pltpu.VMEM((2, slots, kept, HEAD_DIM), jnp.bfloat16),
+            pltpu.VMEM((2, slots, length, HEAD_DIM), jnp.bfloat16),
+            pltpu.VMEM((2, slots, kept, HEAD_DIM), jnp.bfloat16),
+            pltpu.VMEM((slots, length, HEAD_DIM), jnp.bfloat16),
+            pltpu.VMEM((slots, near, length), jnp.float32),
+            pltpu.VMEM((slots, 3, 1, length), jnp.float32),
+            pltpu.VMEM((slots, 3, 1, length), jnp.float32),
+            pltpu.VMEM((kept, HEAD_DIM), jnp.float32),
+            pltpu.VMEM((kept, HEAD_DIM), jnp.float32),
+            sems((2, slots, near - 1)),
+            sems((2, slots, near - 1)),
+            sems((2, slots, count - 1)),
+            sems((2, slots, count - 1)),
+            sems((4, slots)),
+            sems((slots,)),
+            sems((slots,)),
+            sems((2, slots, near - 1)),
+            sems((2, slots, near - 1)),
+            sems((slots, count - 1)),
+            sems((slots, count - 1)),
+            sems((3, slots)),
+        ],
+        compiler_params=pltpu.CompilerParams(
+            collective_id=0, has_side_effects=True, vmem_limit_bytes=64 * 1024 * 1024
+        ),
+    )(key_rows, value_rows, queries, out_grad, vertical.T, slash_offsets.T, counts.T)
+    rows = queries.shape[0]
+    query_grad = dq_parts[:rows].astype(jnp.float32) + dq_parts[rows:].astype(jnp.float32)
+    return query_grad.astype(queries.dtype), key_grad, value_grad
+
+
 def solution(mesh):
+    whole_heads = HEADS % mesh.shape["seq"] == 0
     return jax.shard_map(
-        body,
+        whole_head_body if whole_heads else split_head_body,
         mesh=mesh,
         in_specs=(
             P(("doc", "seq"), None),

time: 753 us -> 93.4 us (0.12)
  the two profiles are of different devices: /device:TPU:1 before, /device:TPU:0 now
where the time goes in v1:
time: 93.4 us; the launch traced here: 93.2 us
  Pallas kernels  88.4 us (95%)
  other arithmetic  2.18 us (2%)
  local copies, waits for them, and re-layouts  2.03 us (2%)
    pallas_call x1, Pallas kernels, whole_head_body(): pl.pallas_call(functools.partial(fused_kernel, count, slots), out_shape=(...  88.4 us
    convert_element_type x1, other arithmetic, whole_head_body(): return (query_grad.astype(queries.dtype), key_grad, value_grad)  2.18 us
    unnamed x6, local copies, waits for them, and re-layouts  2.03 us

profile of v1, /device:TPU:0, one launch (start us, length us, event | category | flops | bytes accessed | tf_op | source)
XLA Modules:
  0.0 93.2 jit_solution(10496923615953393631)
XLA Ops:
  0.6 88.4 %shard_map.94 = (bf16[256,2048]{1,0:T(8,128)(2,1)}, bf16[128,2048]{1,0:T(8,128)(2,1)}, bf16[128,2048]{1,0:T(8,128)(2,1)}) custom-call(bf16[128,2048]{1,0:T(8,128)(2,1)} %k_in.1, bf16[128,2048]{1,0:T(8,128)(2,1)} %v_in.1, bf16[128,2048]{1,0:T(8,128)(2,1)} %q_in.1, bf16[128,2048]{1,0:T(8,128)(2,1)} %d_in.1, s32[6,16]{1,0:T(8,128)} %bitcast.3, ...), custom_call_target="tpu_custom_call" | custom-call | tf_op jit(solution)/shard_map/pallas_call | solution.py:528
  89.0 0.0 copy-start.1
  89.0 2.2 %add_convert_fusion = bf16[128,2048]{1,0:T(8,128)(2,1)} fusion(bf16[256,2048]{1,0:T(8,128)(2,1)} %get-tuple-element.6), kind=kLoop, calls=%fused_computation | loop fusion | flops 1048576 | bytes 1572864 | tf_op jit(solution)/shard_map/convert_element_type | solution.py:562
  91.2 0.0 copy-done.1
  91.2 0.0 copy-start
  91.2 0.8 copy.12
  92.0 0.4 copy-done
  92.4 0.8 copy.13
Async XLA Ops:
  89.0 2.2 %copy-start.1 = (bf16[128,2048]{1,0:T(8,128)(2,1)S(1)}, bf16[128,2048]{1,0:T(8,128)(2,1)}, u32[]{:S(2)}) copy-start(bf16[128,2048]{1,0:T(8,128)(2,1)} %get-tuple-element.13) | copy-start | bytes 1572868
  91.2 1.2 %copy-start = (bf16[128,2048]{1,0:T(8,128)(2,1)S(1)}, bf16[128,2048]{1,0:T(8,128)(2,1)}, u32[]{:S(2)}) copy-start(bf16[128,2048]{1,0:T(8,128)(2,1)} %get-tuple-element.14) | copy-start | bytes 1572868
